TPU v7x, 256 devices: a whole 4x4x8 slice. The times are simulated.
256 devices in a mesh: grp: 16 (over y, x), sp: 16 (over z, core).
Axes of the slice: x: 4, y: 4, z: 8, core: 2. Of those that a mesh axis runs over, the one named last changes fastest.
Arguments:
- latents: bfloat16 [128, 512, 1152], P('grp', 'sp'), may hold values from -6 to 6
- route: int32 [128], replicated, may hold values from 0 to 127, as said below
- counts: int32 [16, 4], P('grp'), may hold values from 1 to 3, 8 in all within a row
- modulation: float32 [64, 3, 1152], P('grp'), may hold values from -4 to 4
- w_qkv: bfloat16 [1152, 3456], replicated, may hold values from -0.1875 to 0.1875
- w_out: bfloat16 [1152, 1152], replicated, may hold values from -0.1875 to 0.1875
- cotangent: bfloat16 [128, 512, 1152], P('grp', 'sp'), may hold values from -6 to 6
Outputs:
- output: bfloat16 [128, 512, 1152], P('grp', 'sp')
- grad_in: bfloat16 [128, 512, 1152], P('grp', 'sp')
Inputs may be any that keep to these rules, and one draw needn't show every extreme that they name: `route`: a permutation; entry g * 8 + s is the balanced slot of frame s of group g, and the balanced slot's group is its value divided by 8; no group hands more than 2 frames to one group, and some pair of groups has exactly 2. `counts`: each group's clips fill its 8 balanced frames in order.
All inputs are finite; a program needn't handle non-finite values.
Results may differ from a plain program's by a relative error of at most 0.03.
Values may be sent and summed in bfloat16 or wider, within the bound.
A program may use at most 128 MiB of HBM per device.

v0:
```python
import functools
import math

import jax
import jax.numpy as jnp
from jax import lax
from jax.experimental import pallas as pl
from jax.experimental.pallas import tpu as pltpu
from jax.sharding import PartitionSpec as P

MESH = pl.DeviceIdType.MESH
HEADS = 16
LANES = 128
EPS = 1e-06
NT = (((1,), (1,)), ((), ()))
NN = (((1,), (0,)), ((), ()))
TN = (((0,), (0,)), ((), ()))
BF = jnp.bfloat16
F32 = jnp.float32


def dot(a, b, dims):
    return lax.dot_general(a, b, dims, preferred_element_type=F32)


def bits_of(number):
    return number.bit_length() - 1


def colour(route_row, groups, frames):
    edges = groups * frames
    shift = bits_of(frames)
    square = (edges, edges)
    r_wide = jnp.broadcast_to(route_row.astype(F32), square)
    r_row, r_col = r_wide.astype(jnp.int32), r_wide.T.astype(jnp.int32)
    k_row = lax.broadcasted_iota(jnp.int32, square, 1)
    k_col = lax.broadcasted_iota(jnp.int32, square, 0)
    same_source = (k_row >> shift) == (k_col >> shift)
    same_target = (r_row >> shift) == (r_col >> shift)
    as_bf = lambda flag: jnp.where(flag, 1.0, 0.0).astype(BF)
    eye = jnp.where(k_row == k_col, 1.0, 0.0)
    c_row = jnp.zeros((1, edges), jnp.int32)
    c_col = jnp.zeros((edges, 1), jnp.int32)
    for level in range(shift):
        same = c_row == c_col
        s_pair = as_bf(same & same_source & ((k_row >> level) == ((k_col >> level) ^ 1)))
        t_pair = as_bf(same & same_target & ((r_row >> level) == ((r_col >> level) ^ 1)))
        reach = (dot(s_pair, t_pair, NN) + dot(t_pair, s_pair, NN) + eye).astype(BF)
        for _ in range(max(1, bits_of(edges) - 2 - level)):
            reach = dot(reach, reach, NN).astype(BF)
        mine = reach > 0
        partner = dot(s_pair, reach, NN) > 0
        first = lambda flag, ids, axis: jnp.min(jnp.where(flag, ids, edges), axis=axis, keepdims=True)
        bit_row = (first(mine, k_col, 0) < first(partner, k_col, 0)).astype(jnp.int32)
        bit_col = (first(mine, k_row, 1) < first(partner, k_row, 1)).astype(jnp.int32)
        c_row = c_row * 2 + bit_row
        c_col = c_col * 2 + bit_col
    return c_col, r_col[:, :1], k_col[:, :1]


def table_starts(groups, frames):
    starts = [0]
    for length in (frames, groups, frames, frames, groups, frames):
        starts.append(starts[-1] + length)
    return starts


def make_table(route_row, groups, frames, me):
    c, r, k = colour(route_row, groups, frames)
    shift = bits_of(frames)
    starts = table_starts(groups, frames)
    t = lax.broadcasted_iota(jnp.int32, (1, LANES), 1)
    source, target = k >> shift, r >> shift
    by_source, by_target = source * frames + c, target * frames + c
    via = me // 2
    runs = [
        (by_target, me * frames + t - starts[0], r & (frames - 1)),
        (by_source, (t - starts[1]) * frames + via, target),
        (k, me * frames + t - starts[2], c),
        (by_source, me * frames + t - starts[3], k & (frames - 1)),
        (by_target, (t - starts[4]) * frames + via, source),
        (r, me * frames + t - starts[5], c),
    ]
    table = jnp.zeros((1, LANES), jnp.int32)
    for i, (key, wanted, value) in enumerate(runs):
        found = jnp.sum(jnp.where(key == wanted, value, 0), axis=0, keepdims=True)
        found = jnp.clip(found, 0, starts[i + 1] - starts[i] - 1)
        table = jnp.where((t >= starts[i]) & (t < starts[i + 1]), found, table)
    return table


def kernel(
    groups,
    route,
    counts,
    route_row,
    lat,
    ct_hbm,
    mod,
    wqkv_hbm,
    wout_hbm,
    out_ref,
    grad_ref,
    wqkv,
    wout,
    ct,
    c1_send,
    c1_recv,
    c2_send,
    c2_recv,
    o1_send,
    o1_recv,
    o2_send,
    o2_recv,
    ct_stage,
    ct_rows,
    out_stage,
    out_mid,
    grad_stage,
    mod_send,
    mod_recv,
    modf,
    x_rows,
    normed,
    qkv,
    qp,
    kp,
    vp,
    probs,
    op,
    att,
    dop,
    inverse,
    dk_own,
    dv_own,
    part_send,
    part_recv,
    tab_row,
    tab,
    w_sem,
    xs,
    xr,
    ms,
    mr,
    c1s,
    c1r,
    c2s,
    c2r,
    czs,
    czr,
    kvs,
    kvr,
    ozs,
    ozr,
    o1s,
    o1r,
    o2s,
    o2r,
    ps,
    pr,
    gs,
    gr,
):
    frames, rows, width = ct_hbm.shape
    head = width // HEADS
    zs = frames
    half = frames * rows
    me = lax.axis_index("grp")
    sp = lax.axis_index("sp")
    z = sp // 2
    core = sp % 2
    starts = table_starts(groups, frames)
    piece = rows // 2

    def z_dev(d):
        return {"sp": lax.rem(z + d, zs) * 2 + core}

    def g_dev(d):
        return {"grp": lax.rem(me + d, groups)}

    other = {"sp": z * 2 + (1 - core)}

    w1 = pltpu.make_async_copy(wqkv_hbm, wqkv, w_sem.at[0])
    w2 = pltpu.make_async_copy(wout_hbm, wout, w_sem.at[1])
    barrier = pltpu.get_barrier_semaphore()
    for d in range(1, zs):
        pl.semaphore_signal(barrier, inc=1, device_id=z_dev(d), device_id_type=MESH)
    for d in range(1, groups):
        pl.semaphore_signal(barrier, inc=1, device_id=g_dev(d), device_id_type=MESH)
    pl.semaphore_signal(barrier, inc=1, device_id=other, device_id_type=MESH)
    ct_c = pltpu.make_async_copy(ct_hbm, ct, w_sem.at[3])
    ct_c.start()
    w1.start()
    w2.start()

    def remote(src, dst, s_sem, r_sem, dev):
        return pltpu.make_async_remote_copy(
            src_ref=src, dst_ref=dst, send_sem=s_sem, recv_sem=r_sem, device_id=dev, device_id_type=MESH
        )

    middle = -(-width // LANES // 2) * LANES
    parts = [pl.ds(0, middle), pl.ds(middle, width - middle)]

    def group_copies(src, dst, s_sem, r_sem):
        def copies(i):
            own = pltpu.make_async_copy(src[i].at[me], dst[i].at[me], s_sem.at[i, 0])
            return [own] + [
                remote(src[i].at[lax.rem(me + d, groups)], dst[i].at[me], s_sem.at[i, d], r_sem.at[i, d], g_dev(d))
                for d in range(1, groups)
            ]

        return [copies(i) for i in range(2)]

    def mod_copies():
        own = pltpu.make_async_copy(mod_send.at[me], mod_recv.at[me], ms.at[0])
        return [own] + [
            remote(mod_send.at[lax.rem(me + d, groups)], mod_recv.at[me], ms.at[d], mr.at[d], g_dev(d))
            for d in range(1, groups)
        ]

    near_first = sorted(range(1, zs), key=lambda d: min(d, zs - d))

    ahead = [0] + [zs - d for d in near_first]

    def to_frames(src, dst, s_sem, r_sem, i, cols):
        own = pltpu.make_async_copy(src.at[z, :, cols], dst.at[0, :, cols], s_sem.at[i, 0])
        return [own] + [
            remote(
                src.at[lax.rem(z + d, zs), :, cols],
                dst.at[n + 1, :, cols],
                s_sem.at[i, d],
                r_sem.at[i, d],
                z_dev(d),
            )
            for n, d in enumerate(near_first)
        ]

    def from_frames(src, dst, s_sem, r_sem, i, cols):
        own = pltpu.make_async_copy(src.at[0, :, cols], dst.at[z], s_sem.at[i, 0])
        return [own] + [
            remote(src.at[n, :, cols], dst.at[z], s_sem.at[i, d], r_sem.at[i, d], z_dev(d))
            for n, d in list(enumerate(ahead))[1:]
        ]

    def start(copies):
        for copy in copies:
            copy.start()

    def wait_recv(copies):
        copies[0].wait()
        for copy in copies[1:]:
            copy.wait_recv()

    def wait_send(copies):
        for copy in copies[1:]:
            copy.wait_send()

    whole = pl.ds(0, width)
    tab_row[...] = make_table(route_row[...], groups, frames, me)
    tab_c = pltpu.make_async_copy(tab_row, tab, w_sem.at[2])
    tab_c.start()

    ends = [counts[0, 0]]
    for i in range(1, counts.shape[1] - 1):
        ends.append(ends[-1] + counts[0, i])
    for g in range(groups):
        slot = lax.rem(route[g * frames + z], frames)
        clip = sum([jnp.where(slot >= end, 1, 0) for end in ends])
        for i in range(3):
            mod_send[g, i : i + 1, :] = mod[i, pl.ds(clip, 1), :]

    tab_c.wait()
    ct_c.wait()

    def spread_frames(source, first, send, cols):
        for m in range(groups):
            send[m] = source[tab[0, first + m // 2], (m % 2) * piece : (m % 2 + 1) * piece, cols]

    def pass_on(received, first, send):
        for g in range(groups):
            send[g] = received[tab[0, first + g]]

    def join_frames(received, first, target, cols):
        for f in range(frames):
            c = tab[0, first + f]
            target[f, :piece, cols] = received[2 * c]
            target[f, piece:, cols] = received[2 * c + 1]

    for i, cols in enumerate(parts):
        spread_frames(ct, starts[0], c1_send[i], cols)
    pl.semaphore_wait(barrier, zs - 1 + groups - 1 + 1)

    x_c = to_frames(lat, x_rows, xs, xr, 0, whole)
    start(x_c)
    c1_c = group_copies(c1_send, c1_recv, c1s, c1r)
    c2_c = group_copies(c2_send, c2_recv, c2s, c2r)
    cz_c = [to_frames(ct_stage, ct_rows, czs, czr, i, cols) for i, cols in enumerate(parts)]
    mod_c = mod_copies()
    start(c1_c[0])
    start(c1_c[1])
    start(mod_c)

    def cotangent_on(i):
        wait_recv(c2_c[i])
        join_frames(c2_recv[i], starts[2], ct_stage, parts[i])
        start(cz_c[i])

    qkv[:, 3 * width :] = jnp.zeros((half, qkv.shape[1] - 3 * width), BF)
    for i in range(2):
        wait_recv(c1_c[i])
        pass_on(c1_recv[i], starts[1], c2_send[i])
        start(c2_c[i])
    wait_recv(mod_c)
    modf[:3, :] = mod_recv[route[me * frames + z] // frames]

    def norm_parts(r):
        x = x_rows[r].astype(F32)
        center = jnp.mean(x, axis=-1, keepdims=True)
        spread = x - center
        inv = lax.rsqrt(jnp.mean(spread * spread, axis=-1, keepdims=True) + EPS)
        return x, spread * inv, inv

    lane = lax.broadcasted_iota(jnp.int32, (half, LANES), 1)

    def arrive(first, last):
        for r in range(first, last):
            x_c[r].wait() if r == 0 else x_c[r].wait_recv()
            _, xhat, _ = norm_parts(r)
            normed[r * rows : (r + 1) * rows, :] = (xhat * (1.0 + modf[1:2, :]) + modf[0:1, :]).astype(BF)

    def project(start_col, stop_col, some):
        for at in range(start_col, stop_col, 256):
            cols = slice(at, min(at + 256, stop_col))
            qkv[some, cols] = dot(normed[some, :], wqkv[:, cols], NN).astype(BF)

    def padded(source, start_col):
        piece = source[:, start_col : start_col + LANES]
        return jnp.where(lane < head, piece, jnp.zeros_like(piece))

    k_c = remote(kp.at[0], kp.at[1], kvs.at[0], kvr.at[0], other)
    v_c = remote(vp.at[0], vp.at[1], kvs.at[1], kvr.at[1], other)
    k_stop = width + -(-width // 256) * 256
    arrive(0, zs // 2)
    w1.wait()
    early, late = slice(0, half // 2), slice(half // 2, half)
    project(width, 3 * width, early)
    project(0, width, early)
    cotangent_on(0)
    arrive(zs // 2, zs)
    project(width, k_stop, late)
    for h in range(HEADS):
        kp[0, :, h * LANES : (h + 1) * LANES] = padded(qkv, width + h * head)
    k_c.start()
    cotangent_on(1)
    project(k_stop, 3 * width, late)
    for h in range(HEADS):
        piece_v = padded(qkv, 2 * width + h * head)
        vp[0, :, h * LANES : (h + 1) * LANES] = jnp.where(lane == head, jnp.ones_like(piece_v), piece_v)
    v_c.start()
    project(0, width, late)
    for h in range(HEADS):
        qp[:, h * LANES : (h + 1) * LANES] = padded(qkv, h * head)
    k_c.wait_recv()
    v_c.wait_recv()

    factor = head**-0.5
    log2 = factor * math.log2(math.e)
    def spot_of(h):
        return pl.ds(h * LANES, LANES)

    def head_keys(ref, h):
        return ref[:, :, spot_of(h)].reshape(2 * half, LANES)

    def scores_of(h):
        return dot(head_keys(kp, h), qp[:, spot_of(h)], NT)

    def attend(h, scores):
        top = jnp.max(scores, axis=0, keepdims=True)
        ex = jnp.exp2((scores - top) * log2).astype(BF)
        probs[h] = ex
        mixed = dot(head_keys(vp, h), ex, TN).T
        inv = 1.0 / mixed[:, head : head + 1]
        inverse[h] = jnp.broadcast_to(inv, (half, LANES))
        op[:, spot_of(h)] = (mixed * inv).astype(BF)

    scores = scores_of(0)
    for h in range(HEADS):
        upcoming = scores_of(h + 1) if h + 1 < HEADS else None
        attend(h, scores)
        scores = upcoming

    for h in range(HEADS):
        att[:, h * head : (h + 1) * head] = op[:, h * LANES : h * LANES + head]

    w2.wait()

    col_tiles = [slice(at, min(at + 256, width)) for at in range(0, width, 256)]
    for cols in col_tiles:
        proj = dot(att[...], wout[:, cols], NN)
        x = x_rows[:, :, cols].astype(F32)
        mixed = modf[2:3, cols] * proj
        out_stage[:, :, cols] = (x + mixed.reshape(x.shape)).astype(BF)
    wait_recv(cz_c[0])
    wait_recv(cz_c[1])
    oz_c = [from_frames(out_stage, out_mid[i], ozs, ozr, i, cols) for i, cols in enumerate(parts)]
    o1_c = group_copies(o1_send, o1_recv, o1s, o1r)
    o2_c = group_copies(o2_send, o2_recv, o2s, o2r)
    start(oz_c[0])
    start(oz_c[1])

    whole_part = slice(None)

    def output_on(i):
        wait_recv(oz_c[i])
        spread_frames(out_mid[i], starts[3], o1_send[i], whole_part)
        start(o1_c[i])

    def gated_step(r, carry):
        normed_rows = pl.ds(r * rows, rows)
        att[normed_rows, :] = (ct_rows[r].astype(F32) * modf[2:3, :]).astype(BF)
        return carry

    lax.fori_loop(0, frames, gated_step, 0)

    for cols in col_tiles:
        qkv[:, cols] = dot(att[...], wout[cols, :], NT).astype(BF)
    for h in range(HEADS):
        dop[:, h * LANES : (h + 1) * LANES] = padded(qkv, h * head)

    segments = part_send.shape[0]
    per = HEADS // segments

    def back_begin(h):
        do = dop[:, spot_of(h)] * inverse[h]
        total = jnp.sum((do * op[:, spot_of(h)]).T, axis=0, keepdims=True)
        do = do.astype(BF)
        return do, total, dot(head_keys(vp, h), do, NT)

    def back_end(h, seg, j, do, total, dp):
        spot = spot_of(h)
        p = probs[h]
        ds = (p * (dp - total)).astype(BF)
        dv = dot(p, do, NN)
        dk = dot(ds, qp[:, spot], NN) * factor
        op[:, spot] = (dot(head_keys(kp, h), ds, TN) * factor).T.astype(BF)
        dk_own[:, spot] = dk[:half]
        dv_own[:, spot] = dv[:half]
        part_send[seg, 0, :, spot_of(j)] = dk[half:].astype(BF)
        part_send[seg, 1, :, spot_of(j)] = dv[half:].astype(BF)

    part_c = []
    for seg in range(segments):
        begun = back_begin(seg * per)
        for j in range(per):
            h = seg * per + j
            upcoming = back_begin(h + 1) if j + 1 < per else None
            back_end(h, seg, j, *begun)
            begun = upcoming
        copy = remote(part_send.at[seg], part_recv.at[seg], ps.at[seg], pr.at[seg], other)
        copy.start()
        part_c.append(copy)
    output_on(0)
    for h in range(HEADS):
        qkv[:, h * head : (h + 1) * head] = op[:, h * LANES : h * LANES + head]
    for seg in range(segments):
        part_c[seg].wait_recv()
        for j in range(per):
            h = seg * per + j
            spot = slice(h * LANES, (h + 1) * LANES)
            there = slice(j * LANES, (j + 1) * LANES)
            dk = (dk_own[:, spot] + part_recv[seg, 0, :, there].astype(F32)).astype(BF)
            dv = (dv_own[:, spot] + part_recv[seg, 1, :, there].astype(F32)).astype(BF)
            qkv[:, width + h * head : width + (h + 1) * head] = dk[:, :head]
            qkv[:, 2 * width + h * head : 2 * width + (h + 1) * head] = dv[:, :head]

    for cols in col_tiles:
        att[:, cols] = dot(qkv[:, : 3 * width], wqkv[cols, :], NT).astype(BF)

    output_on(1)

    gz_c = from_frames(grad_stage, grad_ref, gs, gr, 0, whole)
    for r in range(zs):
        _, xhat, inv = norm_parts(r)
        dhat = att[r * rows : (r + 1) * rows, :].astype(F32) * (1.0 + modf[1:2, :])
        m1 = jnp.mean(dhat, axis=-1, keepdims=True)
        m2 = jnp.mean(dhat * xhat, axis=-1, keepdims=True)
        grad_stage[r] = (ct_rows[r].astype(F32) + inv * (dhat - m1 - xhat * m2)).astype(BF)
        gz_c[r].start()

    for i in range(2):
        wait_recv(o1_c[i])
        pass_on(o1_recv[i], starts[4], o2_send[i])
        start(o2_c[i])
    for i, cols in enumerate(parts):
        wait_recv(o2_c[i])
        join_frames(o2_recv[i], starts[5], out_ref, cols)
    wait_recv(gz_c)

    for copies in [x_c, mod_c, gz_c] + c1_c + c2_c + cz_c + oz_c + o1_c + o2_c:
        wait_send(copies)
    k_c.wait_send()
    v_c.wait_send()
    for copy in part_c:
        copy.wait_send()


def place(out_from, grad_from, out_ref, grad_ref, held, in_sem, out_sem):
    arrays = [(out_from, out_ref), (grad_from, grad_ref)]
    spots = [(n, i) for i in range(out_ref.shape[0]) for n in range(2)]
    come = [pltpu.make_async_copy(arrays[n][0].at[i], held.at[n, i], in_sem.at[n, i]) for n, i in spots]
    go = [pltpu.make_async_copy(held.at[n, i], arrays[n][1].at[i], out_sem.at[n, i]) for n, i in spots]
    for copy in come:
        copy.start()
    for before, after in zip(come, go):
        before.wait()
        after.start()
    for copy in go:
        copy.wait()


def local(latents, route, counts, modulation, w_qkv, w_out, cotangent):
    frames, rows, width = latents.shape
    groups = lax.axis_size("grp")
    half = frames * rows
    padded = HEADS * LANES
    segments = 2
    piece = (frames, rows, width)
    middle = -(-width // LANES // 2) * LANES
    widths = (middle, width - middle)
    dma = pltpu.SemaphoreType.DMA
    vmem = pltpu.VMEM
    block = jax.ShapeDtypeStruct(piece, BF)
    scratch = [vmem(w_qkv.shape, BF), vmem(w_out.shape, BF), vmem(piece, BF)]
    scratch += [tuple(vmem((groups, rows // 2, some), BF) for some in widths)] * 8
    scratch += [vmem(piece, BF)] * 3 + [tuple(vmem((frames, rows, some), BF) for some in widths), vmem(piece, BF)]
    scratch += [vmem((groups, 3, width), F32)] * 2
    scratch += [
        vmem((8, width), F32),
        vmem(piece, BF),
        vmem((half, width), BF),
        vmem((half, 3 * width + LANES), BF),
        vmem((half, padded), BF),
        vmem((2, half, padded), BF),
        vmem((2, half, padded), BF),
        vmem((HEADS, 2 * half, half), BF),
        vmem((half, padded), BF),
        vmem((half, width), BF),
        vmem((half, padded), BF),
        vmem((HEADS, half, LANES), F32),
        vmem((half, padded), F32),
        vmem((half, padded), F32),
        vmem((segments, 2, half, padded // segments), BF),
        vmem((segments, 2, half, padded // segments), BF),
        vmem((1, LANES), jnp.int32),
        pltpu.SMEM((1, LANES), jnp.int32),
        dma((4,)),
    ]
    along_z, across = dma((2, frames)), dma((2, groups))
    scratch += [along_z] * 2 + [dma((groups,))] * 2 + [across] * 4 + [along_z] * 2 + [dma((2,))] * 2
    scratch += [along_z] * 2 + [across] * 4 + [dma((segments,))] * 2 + [along_z] * 2
    in_vmem = pl.BlockSpec(memory_space=vmem)
    in_smem = pl.BlockSpec(memory_space=pltpu.SMEM)
    anywhere = pl.BlockSpec(memory_space=pl.ANY)
    results = pl.pallas_call(
        functools.partial(kernel, groups),
        out_shape=(block, block),
        in_specs=[in_smem, in_smem, in_vmem, anywhere, anywhere, in_vmem, anywhere, anywhere],
        out_specs=(in_vmem, in_vmem),
        scratch_shapes=scratch,
        compiler_params=pltpu.CompilerParams(
            collective_id=0, has_side_effects=True, vmem_limit_bytes=60 * 1024 * 1024
        ),
    )(route, counts, route.reshape(1, -1), latents, cotangent, modulation.transpose(1, 0, 2), w_qkv, w_out)
    return pl.pallas_call(
        place,
        out_shape=(block, block),
        in_specs=[anywhere, anywhere],
        out_specs=(anywhere, anywhere),
        scratch_shapes=[vmem((2,) + piece, BF), dma((2, frames)), dma((2, frames))],
        compiler_params=pltpu.CompilerParams(vmem_limit_bytes=60 * 1024 * 1024),
    )(*results)


def solution(mesh):
    rows = P("grp", "sp", None)
    return jax.shard_map(
        local,
        mesh=mesh,
        in_specs=(rows, P(), P("grp", None), P("grp", None, None), P(), P(), rows),
        out_specs=(rows, rows),
        check_vma=False,
    )
```

profile of v0, /device:TPU:32, one launch (start us, length us, event | category | flops | bytes accessed | tf_op | source)
XLA Modules:
  0.0 77.6 jit_solution(10103500288683579419)
XLA Ops:
  0.6 74.5 %shard_map.86 = (bf16[8,32,1152]{2,1,0:T(8,128)(2,1)}, bf16[8,32,1152]{2,1,0:T(8,128)(2,1)}) custom-call(s32[128]{0:T(128)} %route.1, s32[1,4]{1,0:T(1,128)} %counts.1, s32[1,128]{1,0:T(1,128)} %bitcast.3, bf16[8,32,1152]{2,1,0:T(8,128)(2,1)} %lat.1, bf16[8,32,1152]{2,1,0:T(8,128)(2,1)} %ct_hbm.1, f32[3,4,1152]{2,1,0:T(4,128)} %bitcast.2, ...), custom_call_target="tpu_custom_call" | custom-call | tf_op jit(solution)/shard_map/pallas_call | solution.py:564
  75.2 2.3 %shard_map.87 = (bf16[8,32,1152]{2,1,0:T(8,128)(2,1)}, bf16[8,32,1152]{2,1,0:T(8,128)(2,1)}) custom-call(bf16[8,32,1152]{2,1,0:T(8,128)(2,1)} %get-tuple-element.4.out_from, bf16[8,32,1152]{2,1,0:T(8,128)(2,1)} %get-tuple-element.5.grad_from), custom_call_target="tpu_custom_call" | custom-call | tf_op jit(solution)/shard_map/pallas_call | solution.py:574
where the time goes:
time: 78.6 us; the launch traced here: 77.6 us
  Pallas kernels  76.8 us (98%)
  between operations  0.8 us (1%)
    pallas_call x1, Pallas kernels, local(): pl.pallas_call(functools.partial(kernel, groups), out_shape=(block, block...  74.5 us
    pallas_call x1, Pallas kernels, local(): pl.pallas_call(place, out_shape=(block, block), in_specs=[anywhere, anywh...  2.26 us

commit v1 on v0

--- a/solution.py
+++ b/solution.py
@@ -406,7 +406,6 @@
     o1_c = group_copies(o1_send, o1_recv, o1s, o1r)
     o2_c = group_copies(o2_send, o2_recv, o2s, o2r)
     start(oz_c[0])
-    start(oz_c[1])
 
     whole_part = slice(None)
 
@@ -427,6 +426,7 @@
     for h in range(HEADS):
         dop[:, h * LANES : (h + 1) * LANES] = padded(qkv, h * head)
 
+    start(oz_c[1])
     segments = part_send.shape[0]
     per = HEADS // segments
 

time: 78.6 us -> 78.5 us (level)
  no operation moved by 1% of the time
where the time goes in v1:
time: 78.5 us; the launch traced here: 77.6 us
  Pallas kernels  76.8 us (98%)
  between operations  0.8 us (1%)
    pallas_call x1, Pallas kernels, local(): pl.pallas_call(functools.partial(kernel, groups), out_shape=(block, block...  74.5 us
    pallas_call x1, Pallas kernels, local(): pl.pallas_call(place, out_shape=(block, block), in_specs=[anywhere, anywh...  2.26 us

profile of v1, /device:TPU:32, one launch (start us, length us, event | category | flops | bytes accessed | tf_op | source)
XLA Modules:
  0.0 77.6 jit_solution(5457595390654677120)
XLA Ops:
  0.6 74.5 %shard_map.86 = (bf16[8,32,1152]{2,1,0:T(8,128)(2,1)}, bf16[8,32,1152]{2,1,0:T(8,128)(2,1)}) custom-call(s32[128]{0:T(128)} %route.1, s32[1,4]{1,0:T(1,128)} %counts.1, s32[1,128]{1,0:T(1,128)} %bitcast.3, bf16[8,32,1152]{2,1,0:T(8,128)(2,1)} %lat.1, bf16[8,32,1152]{2,1,0:T(8,128)(2,1)} %ct_hbm.1, f32[3,4,1152]{2,1,0:T(4,128)} %bitcast.2, ...), custom_call_target="tpu_custom_call" | custom-call | tf_op jit(solution)/shard_map/pallas_call | solution.py:564
  75.1 2.3 %shard_map.87 = (bf16[8,32,1152]{2,1,0:T(8,128)(2,1)}, bf16[8,32,1152]{2,1,0:T(8,128)(2,1)}) custom-call(bf16[8,32,1152]{2,1,0:T(8,128)(2,1)} %get-tuple-element.4.out_from, bf16[8,32,1152]{2,1,0:T(8,128)(2,1)} %get-tuple-element.5.grad_from), custom_call_target="tpu_custom_call" | custom-call | tf_op jit(solution)/shard_map/pallas_call | solution.py:574

commit v2 on v1

--- a/solution.py
+++ b/solution.py
@@ -476,7 +476,6 @@
     for cols in col_tiles:
         att[:, cols] = dot(qkv[:, : 3 * width], wqkv[cols, :], NT).astype(BF)
 
-    output_on(1)
 
     gz_c = from_frames(grad_stage, grad_ref, gs, gr, 0, whole)
     for r in range(zs):
@@ -488,6 +487,8 @@
         gz_c[r].start()
 
     for i in range(2):
+        if i == 1:
+            output_on(1)
         wait_recv(o1_c[i])
         pass_on(o1_recv[i], starts[4], o2_send[i])
         start(o2_c[i])

time: 78.5 us -> 81.2 us (1.034)
  Pallas kernels: 76.8 us -> 80.2 us
    pallas_call x1, Pallas kernels: 74.5 us -> 78 us  [local(): pl.pallas_call(functools.partial(kernel, groups), out_shape=(block, block...]
where the time goes in v2:
time: 81.2 us; the launch traced here: 81 us
  Pallas kernels  80.2 us (99%)
    pallas_call x1, Pallas kernels, local(): pl.pallas_call(functools.partial(kernel, groups), out_shape=(block, block...  78 us
    pallas_call x1, Pallas kernels, local(): pl.pallas_call(place, out_shape=(block, block), in_specs=[anywhere, anywh...  2.26 us

profile of v2, /device:TPU:32, one launch (start us, length us, event | category | flops | bytes accessed | tf_op | source)
XLA Modules:
  0.0 81.0 jit_solution(9582360894428685160)
XLA Ops:
  0.6 78.0 %shard_map.86 = (bf16[8,32,1152]{2,1,0:T(8,128)(2,1)}, bf16[8,32,1152]{2,1,0:T(8,128)(2,1)}) custom-call(s32[128]{0:T(128)} %route.1, s32[1,4]{1,0:T(1,128)} %counts.1, s32[1,128]{1,0:T(1,128)} %bitcast.3, bf16[8,32,1152]{2,1,0:T(8,128)(2,1)} %lat.1, bf16[8,32,1152]{2,1,0:T(8,128)(2,1)} %ct_hbm.1, f32[3,4,1152]{2,1,0:T(4,128)} %bitcast.2, ...), custom_call_target="tpu_custom_call" | custom-call | tf_op jit(solution)/shard_map/pallas_call | solution.py:565
  78.6 2.3 %shard_map.87 = (bf16[8,32,1152]{2,1,0:T(8,128)(2,1)}, bf16[8,32,1152]{2,1,0:T(8,128)(2,1)}) custom-call(bf16[8,32,1152]{2,1,0:T(8,128)(2,1)} %get-tuple-element.4.out_from, bf16[8,32,1152]{2,1,0:T(8,128)(2,1)} %get-tuple-element.5.grad_from), custom_call_target="tpu_custom_call" | custom-call | tf_op jit(solution)/shard_map/pallas_call | solution.py:575
